TPU v7x, 128 devices: a whole 4x4x4 slice. The times are simulated.
128 devices in a mesh: row: 16 (over x, y), col: 8 (over z, core).
Axes of the slice: x: 4, y: 4, z: 4, core: 2. Of those that a mesh axis runs over, the one named last changes fastest.
Arguments:
- out_grad: bfloat16 [16384, 2880], P(('row', 'col')), may hold values from -6 to 6
- tokens: bfloat16 [16384, 2880], P(('row', 'col')), may hold values from -6 to 6
- expert_ids: int32 [16384, 4], P(('row', 'col')), may hold values from 0 to 127, all different within a row; in each aligned block of 128 rows (0 to 127, 128 to 255, ...) at most 5 rows name the same one
- gates: float32 [16384, 4], P(('row', 'col')), may hold values from 0.05 to 1
- w_gate_up: bfloat16 [128, 2880, 2880], P(('row', 'col')), may hold values from -0.109375 to 0.109375
- w_down: bfloat16 [128, 1440, 2880], P(('row', 'col')), may hold values from -0.15625 to 0.15625
Outputs:
- input_grad: bfloat16 [16384, 2880], P(('row', 'col'))
- route_grad: float32 [16384, 4], P(('row', 'col'))
Inputs may be any that keep to these rules, and one draw needn't show every extreme that they name: `expert_ids`: A token's 4 experts differ; among the tokens of one device no expert is named more than 5 times, and in some device some expert is named exactly 5 times.
All inputs are finite; a program needn't handle non-finite values.
Results may differ from a plain program's by a relative error of at most 0.008.
Values may be sent and summed in bfloat16 or wider, within the bound.
A program may use at most 128 MiB of HBM per device.

v0:
```python
import jax
import jax.numpy as jnp
from jax import lax
from jax.sharding import PartitionSpec as P

swish_alpha = 1.702


def shards(out_grad, tokens, expert_ids, gates, w_gate_up, w_down):
    row_count = lax.axis_size("row")
    col_count = lax.axis_size("col")
    devices = row_count * col_count
    local_experts = w_down.shape[0]
    hidden_units = w_down.shape[1]
    experts = local_experts * devices
    token_count = out_grad.shape[0]
    model_width = out_grad.shape[1]
    top_routes = expert_ids.shape[1]
    capacity = 5 * top_routes * token_count // (4 * experts)
    flat_ids = expert_ids.reshape(-1)
    onehot = (flat_ids[:, None] == jnp.arange(experts, dtype=jnp.int32)[None, :]).astype(jnp.int32)
    before = jnp.cumsum(onehot, axis=0) - onehot
    position = jnp.sum(before * onehot, axis=1)
    slot_index = flat_ids * capacity + position
    slot_table = jnp.arange(experts * capacity, dtype=jnp.int32)[:, None] == slot_index[None, :]
    dispatch = jnp.any(
        slot_table.reshape(experts * capacity, token_count, top_routes), axis=2
    ).astype(jnp.bfloat16)
    stacked = jnp.concatenate([out_grad, tokens], axis=1)
    packed = jnp.dot(dispatch, stacked, preferred_element_type=jnp.float32).astype(jnp.bfloat16)
    outgoing = packed.reshape(row_count, col_count, local_experts, capacity, 2 * model_width)
    incoming = lax.all_to_all(
        lax.all_to_all(outgoing, "row", split_axis=0, concat_axis=0, tiled=True),
        "col",
        split_axis=1,
        concat_axis=1,
        tiled=True,
    )
    slot_rows = incoming.reshape(devices, local_experts, capacity, 2 * model_width)
    sources = slot_rows.shape[0]
    slots_held = slot_rows.shape[2]
    grouped = jnp.swapaxes(slot_rows, 0, 1).reshape(local_experts, -1, 2 * model_width)
    grad_rows = grouped[:, :, :model_width]
    input_rows = grouped[:, :, model_width:]
    projected = jnp.einsum(
        "emd,edf->emf", input_rows, w_gate_up, preferred_element_type=jnp.float32
    )
    gate_pre = projected[:, :, :hidden_units]
    up_pre = projected[:, :, hidden_units:]
    hidden_grad = jnp.einsum("emd,efd->emf", grad_rows, w_down, preferred_element_type=jnp.float32)
    sigmoid_gate = jax.nn.sigmoid(swish_alpha * gate_pre)
    activated = gate_pre * sigmoid_gate
    hidden = (up_pre + 1.0) * activated
    route_term = jnp.sum(hidden_grad * hidden, axis=2)
    gate_grad = (
        hidden_grad
        * (up_pre + 1.0)
        * sigmoid_gate
        * (1.0 + swish_alpha * gate_pre * (1.0 - sigmoid_gate))
    )
    up_grad = hidden_grad * activated
    pre_grad = jnp.concatenate([gate_grad, up_grad], axis=2).astype(jnp.bfloat16)
    part_grad = jnp.einsum(
        "emf,edf->emd", pre_grad, w_gate_up, preferred_element_type=jnp.float32
    ).astype(jnp.bfloat16)
    part_back = jnp.swapaxes(
        part_grad.reshape(local_experts, sources, slots_held, model_width), 0, 1
    )
    route_back = jnp.swapaxes(route_term.reshape(local_experts, sources, slots_held), 0, 1)
    part_back, route_back = (part_back, route_back)
    part_back = part_back.reshape(row_count, col_count, local_experts, capacity, model_width)
    route_back = route_back.reshape(row_count, col_count, local_experts, capacity)
    part_home, route_home = (
        lax.all_to_all(
            lax.all_to_all(part_back, "col", split_axis=1, concat_axis=1, tiled=True),
            "row",
            split_axis=0,
            concat_axis=0,
            tiled=True,
        ),
        lax.all_to_all(
            lax.all_to_all(
                route_back.astype(jnp.bfloat16), "col", split_axis=1, concat_axis=1, tiled=True
            ),
            "row",
            split_axis=0,
            concat_axis=0,
            tiled=True,
        ).astype(route_back.dtype),
    )
    part_flat = part_home.reshape(experts * capacity, model_width)
    route_flat = route_home.reshape(experts * capacity)
    picked = part_flat[slot_index].reshape(token_count, top_routes, model_width)
    input_grad = jnp.sum(gates[:, :, None] * picked.astype(jnp.float32), axis=1).astype(
        jnp.bfloat16
    )
    route_grad = route_flat[slot_index].reshape(token_count, top_routes)
    return (input_grad, route_grad)


def solution(mesh):
    placed = (
        P(("row", "col"), None),
        P(("row", "col"), None),
        P(("row", "col"), None),
        P(("row", "col"), None),
        P(("row", "col"), None, None),
        P(("row", "col"), None, None),
    )
    return jax.shard_map(
        shards,
        mesh=mesh,
        in_specs=placed,
        out_specs=(P(("row", "col"), None), P(("row", "col"), None)),
        check_vma=False,
    )
```

profile of v0, /device:TPU:5, one launch (start us, length us, event | category | flops | bytes accessed | tf_op | source)
XLA Modules:
  0.0 460.1 jit_solution(10118396059584061227)
XLA Ops:
  0.6 0.8 copy.37
  1.4 0.1 eq.44
  1.5 0.1 eq.40
  1.6 0.1 copy.40
  1.7 0.2 fusion.28
  2.1 0.2 fusion.27
  2.3 0.1 reduce_sum.32
  2.4 0.1 copy.42
  2.5 0.2 fusion.25
  2.7 6.4 %convolution_convert_fusion = bf16[640,5760]{1,0:T(8,128)(2,1)} fusion(pred[640,128]{1,0:T(8,128)(4,1)S(1)} %fusion.25, bf16[128,2880]{0,1:T(8,128)(2,1)} %param.7, bf16[128,2880]{0,1:T(8,128)(2,1)} %param.6), kind=kOutput, calls=%fused_computation.6 | convolution fusion | flops 950353920 | bytes 8929280 | tf_op jit(solution)/shard_map/dot_general | solution.py:30
  9.1 13.6 %reshape.134 = bf16[16,8,1,5,5760]{4,3,1,0,2:T(8,128)(2,1)} reshape(bf16[640,5760]{1,0:T(8,128)(2,1)} %convolution_convert_fusion) | data formatting | bytes 14745600 | tf_op jit(solution)/shard_map/reshape | solution.py:31
  22.7 8.3 %copy.43 = bf16[16,8,1,5,5760]{4,1,3,2,0:T(8,128)(2,1)} copy(bf16[16,8,1,5,5760]{4,3,1,0,2:T(8,128)(2,1)} %reshape.134) | data formatting | bytes 14745600 | tf_op jit(solution)/shard_map/reshape | solution.py:31
  31.0 90.0 %all_to_all.30 = bf16[16,8,1,5,5760]{4,1,3,2,0:T(8,128)(2,1)S(1)} all-to-all(bf16[16,8,1,5,5760]{4,1,3,2,0:T(8,128)(2,1)} %copy.43), channel_id=1, replica_groups=mesh['row'=16,'col'=8] {'row'}, dimensions={0} | all-to-all | bytes 14745600 | tf_op jit(solution)/shard_map/all_to_all | solution.py:33
  121.0 3.7 copy.44
  124.7 90.8 %all_to_all.31 = bf16[16,8,1,5,5760]{4,0,3,2,1:T(8,128)(2,1)} all-to-all(bf16[16,8,1,5,5760]{4,0,3,2,1:T(8,128)(2,1)} %copy.44), channel_id=1, replica_groups=mesh['row'=16,'col'=8] {'col'}, dimensions={1} | all-to-all | bytes 14745600 | tf_op jit(solution)/shard_map/all_to_all | solution.py:32
  215.5 9.8 %copy.45 = bf16[16,8,1,5,5760]{4,3,1,0,2:T(8,128)(2,1)} copy(bf16[16,8,1,5,5760]{4,0,3,2,1:T(8,128)(2,1)} %all_to_all.31) | data formatting | bytes 14745600 | tf_op jit(solution)/shard_map/all_to_all | solution.py:32
  225.4 13.7 %reshape_transpose_reshape.7 = bf16[1,640,5760]{2,1,0:T(8,128)(2,1)} reshape(bf16[16,8,1,5,5760]{4,3,1,0,2:T(8,128)(2,1)} %copy.45) | data formatting | bytes 14745600 | tf_op jit(solution)/shard_map/reshape;transpose;reshape | solution.py:42
  239.1 19.6 %fusion.6 = f32[1,640,2880]{1,2,0:T(8,128)S(1)} fusion(bf16[1,2880,2880]{2,1,0:T(8,128)(2,1)} %param.10, bf16[1,640,5760]{2,1,0:T(8,128)(2,1)} %reshape_transpose_reshape.7), kind=kOutput, calls=%fused_computation.10 | convolution fusion | flops 10616832000 | bytes 28098560 | tf_op jit(solution)/shard_map/emd,edf->emf/dot_general | solution.py:45
  258.7 0.0 copy-done
  258.7 11.8 %fusion.19 = (bf16[640]{0:T(1024)(128)(2,1)S(1)}, bf16[640,1440]{0,1:T(8,128)(2,1)S(1)}, bf16[640,1440]{0,1:T(8,128)(2,1)}) fusion(f32[1,640,2880]{1,2,0:T(8,128)S(1)} %fusion.6, bf16[1,1440,2880]{2,1,0:T(8,128)(2,1)} %param.11, bf16[1,640,5760]{2,1,0:T(8,128)(2,1)S(1)} %copy-done), kind=kOutput, calls=%fused_computation.25 | convolution fusion | flops 5325004288 | bytes 23123200 | tf_op jit(solution)/shard_map/emd,efd->emf/dot_general | solution.py:50
  270.5 0.2 convert_element_type.51
  270.7 0.8 copy.50
  271.5 4.1 all-to-all-start.4
  275.5 18.3 %fusion.9 = bf16[640,2880]{0,1:T(8,128)(2,1)} fusion(bf16[1,2880,2880]{2,1,0:T(8,128)(2,1)} %param.10, bf16[640,1440]{0,1:T(8,128)(2,1)S(1)} %get-tuple-element.9, bf16[640,1440]{0,1:T(8,128)(2,1)} %get-tuple-element.10), kind=kOutput, calls=%fused_computation.11 | convolution fusion | flops 10626048000 | bytes 23961600 | tf_op jit(solution)/shard_map/emf,edf->emd/dot_general | solution.py:63
  293.8 6.2 %copy.46 = bf16[640,2880]{1,0:T(8,128)(2,1)} copy(bf16[640,2880]{0,1:T(8,128)(2,1)} %fusion.9) | data formatting | bytes 7372800 | tf_op jit(solution)/shard_map/convert_element_type | solution.py:65
  300.0 7.4 %reshape_transpose_reshape.8 = bf16[16,8,1,5,2880]{4,3,1,0,2:T(8,128)(2,1)} reshape(bf16[640,2880]{1,0:T(8,128)(2,1)} %copy.46) | data formatting | bytes 7372800 | tf_op jit(solution)/shard_map/reshape;transpose;reshape | solution.py:71
  307.4 7.1 %copy.47 = bf16[16,8,1,5,2880]{4,0,3,2,1:T(8,128)(2,1)} copy(bf16[16,8,1,5,2880]{4,3,1,0,2:T(8,128)(2,1)} %reshape_transpose_reshape.8) | data formatting | bytes 7372800 | tf_op jit(solution)/shard_map/reshape;transpose;reshape | solution.py:71
  314.5 0.0 all-to-all-done.4
  314.5 4.8 %all-to-all-start.2 = ((bf16[16,8,1,5,2880]{4,0,3,2,1:T(8,128)(2,1)}), bf16[16,8,1,5,2880]{4,0,3,2,1:T(8,128)(2,1)}, u32[]{:S(2)}, u32[]{:S(2)}) async-start(bf16[16,8,1,5,2880]{4,0,3,2,1:T(8,128)(2,1)} %copy.47), calls=%async_computation.2 | async-start | bytes 7536640 | tf_op jit(solution)/shard_map/all_to_all | solution.py:75
  319.3 0.8 copy.51
  320.0 43.6 %all-to-all-done.2 = bf16[16,8,1,5,2880]{4,0,3,2,1:T(8,128)(2,1)} async-done(((bf16[16,8,1,5,2880]{4,0,3,2,1:T(8,128)(2,1)}), bf16[16,8,1,5,2880]{4,0,3,2,1:T(8,128)(2,1)}, u32[]{:S(2)}, u32[]{:S(2)}) %all-to-all-start.2) | async-done | bytes 3686432 | tf_op jit(solution)/shard_map/all_to_all | solution.py:75
  363.6 5.3 %all-to-all-start.5 = ((bf16[16,8,1,5]{3,1,2,0:T(8,128)(2,1)}), bf16[16,8,1,5]{3,1,2,0:T(8,128)(2,1)S(1)}, u32[]{:S(2)}, u32[]{:S(2)}) async-start(bf16[16,8,1,5]{3,1,2,0:T(8,128)(2,1)} %copy.51), calls=%async_computation.5 | async-start | bytes 65536 | tf_op jit(solution)/shard_map/all_to_all | solution.py:81
  369.0 4.6 %copy.48 = bf16[16,8,1,5,2880]{4,1,3,2,0:T(8,128)(2,1)} copy(bf16[16,8,1,5,2880]{4,0,3,2,1:T(8,128)(2,1)} %all-to-all-done.2) | data formatting | bytes 7372800 | tf_op jit(solution)/shard_map/all_to_all | solution.py:75
  373.6 0.0 all-to-all-done.5
  373.6 6.8 %all-to-all-start.3 = ((bf16[16,8,1,5,2880]{4,1,3,2,0:T(8,128)(2,1)}), bf16[16,8,1,5,2880]{4,1,3,2,0:T(8,128)(2,1)}, u32[]{:S(2)}, u32[]{:S(2)}) async-start(bf16[16,8,1,5,2880]{4,1,3,2,0:T(8,128)(2,1)} %copy.48), calls=%async_computation.3 | async-start | bytes 7536640 | tf_op jit(solution)/shard_map/all_to_all | solution.py:74
  380.4 0.1 mul.70
  380.6 0.1 copy.36
  380.7 0.2 reshape.145
  380.9 2.3 gather_fusion.1
  383.2 0.1 reshape.142
  383.3 0.7 copy.53
  384.0 42.2 %all-to-all-done.3 = bf16[16,8,1,5,2880]{4,1,3,2,0:T(8,128)(2,1)} async-done(((bf16[16,8,1,5,2880]{4,1,3,2,0:T(8,128)(2,1)}), bf16[16,8,1,5,2880]{4,1,3,2,0:T(8,128)(2,1)}, u32[]{:S(2)}, u32[]{:S(2)}) %all-to-all-start.3) | async-done | bytes 3686432 | tf_op jit(solution)/shard_map/all_to_all | solution.py:74
  426.2 5.8 %copy.49 = bf16[16,8,1,5,2880]{4,3,1,0,2:T(8,128)(2,1)} copy(bf16[16,8,1,5,2880]{4,1,3,2,0:T(8,128)(2,1)} %all-to-all-done.3) | data formatting | bytes 7372800 | tf_op jit(solution)/shard_map/all_to_all | solution.py:74
  432.0 8.0 %reshape.139 = bf16[640,2880]{1,0:T(8,128)(2,1)} reshape(bf16[16,8,1,5,2880]{4,3,1,0,2:T(8,128)(2,1)} %copy.49) | data formatting | bytes 7372800 | tf_op jit(solution)/shard_map/reshape | solution.py:91
  440.0 8.4 %gather_fusion = bf16[512,2880]{1,0:T(8,128)(2,1)S(1)} fusion(bf16[640,2880]{1,0:T(8,128)(2,1)} %reshape.139, s32[1024]{0:T(1024)S(1)} %pad_clamp_fusion), kind=kCustom, calls=%fused_computation | custom fusion | bytes 5900288 | tf_op jit(solution)/shard_map/gather | solution.py:93
  448.4 3.6 reshape.143
  451.9 7.1 %multiply_reduce_fusion = bf16[128,2880]{1,0:T(8,128)(2,1)S(1)} fusion(f32[128,4,2880]{2,1,0:T(4,128)} %reshape.143, f32[128,4]{1,0:T(8,128)S(1)} %copy.36), kind=kLoop, calls=%fused_computation.9 | loop fusion | flops 2580480 | bytes 6637568 | tf_op jit(solution)/shard_map/reduce_sum | solution.py:94
  459.0 1.1 copy.52
  (12 shorter events, 0.1 us)
Async XLA Ops:
  239.1 19.6 %copy-start = (bf16[1,640,5760]{2,1,0:T(8,128)(2,1)S(1)}, bf16[1,640,5760]{2,1,0:T(8,128)(2,1)}, u32[]{:S(2)}) copy-start(bf16[1,640,5760]{2,1,0:T(8,128)(2,1)} %reshape_transpose_reshape.7) | copy-start | bytes 22118404
  271.5 43.0 %all-to-all-start.4 = ((bf16[16,8,1,5]{0,3,2,1:T(8,128)(2,1)}), bf16[16,8,1,5]{0,3,2,1:T(8,128)(2,1)S(1)}, u32[]{:S(2)}, u32[]{:S(2)}) async-start(bf16[16,8,1,5]{0,3,2,1:T(8,128)(2,1)} %copy.50), calls=%async_computation.4 | async-start | bytes 32768 | tf_op jit(solution)/shard_map/all_to_all | solution.py:82
  314.5 49.2 %all-to-all-start.2 = ((bf16[16,8,1,5,2880]{4,0,3,2,1:T(8,128)(2,1)}), bf16[16,8,1,5,2880]{4,0,3,2,1:T(8,128)(2,1)}, u32[]{:S(2)}, u32[]{:S(2)}) async-start(bf16[16,8,1,5,2880]{4,0,3,2,1:T(8,128)(2,1)} %copy.47), calls=%async_computation.2 | async-start | bytes 7536640 | tf_op jit(solution)/shard_map/all_to_all | solution.py:75
  363.6 10.0 %all-to-all-start.5 = ((bf16[16,8,1,5]{3,1,2,0:T(8,128)(2,1)}), bf16[16,8,1,5]{3,1,2,0:T(8,128)(2,1)S(1)}, u32[]{:S(2)}, u32[]{:S(2)}) async-start(bf16[16,8,1,5]{3,1,2,0:T(8,128)(2,1)} %copy.51), calls=%async_computation.5 | async-start | bytes 65536 | tf_op jit(solution)/shard_map/all_to_all | solution.py:81
  373.6 6.9 %copy-start.1 = (f32[128,4]{0,1:T(4,128)S(1)}, f32[128,4]{0,1:T(4,128)}, u32[]{:S(2)}) copy-start(f32[128,4]{0,1:T(4,128)} %param.9) | copy-start | bytes 6148
  373.6 52.5 %all-to-all-start.3 = ((bf16[16,8,1,5,2880]{4,1,3,2,0:T(8,128)(2,1)}), bf16[16,8,1,5,2880]{4,1,3,2,0:T(8,128)(2,1)}, u32[]{:S(2)}, u32[]{:S(2)}) async-start(bf16[16,8,1,5,2880]{4,1,3,2,0:T(8,128)(2,1)} %copy.48), calls=%async_computation.3 | async-start | bytes 7536640 | tf_op jit(solution)/shard_map/all_to_all | solution.py:74
where the time goes:
time: 467 us; the launch traced here: 460 us
  blocking collectives  181 us (39%)
  local copies, waits for them, and re-layouts  108 us (23%)
  waiting for transfers between devices  85.8 us (18%)
  matrix products  56.1 us (12%)
  starting transfers between devices  21 us (4%)
  other arithmetic  7.76 us (2%)
    all_to_all x1, blocking collectives, shards(): lax.all_to_all(lax.all_to_all(outgoing, 'row', split_axis=0, concat_axis=...  90.8 us
    all_to_all x1, blocking collectives, shards(): lax.all_to_all(outgoing, 'row', split_axis=0, concat_axis=0, tiled=True)  90 us
    all_to_all x1, waiting for transfers between devices, shards(): lax.all_to_all(part_back, 'col', split_axis=1, concat_axis=1, tiled=True)  43.6 us
    all_to_all x1, waiting for transfers between devices, shards(): lax.all_to_all(lax.all_to_all(part_back, 'col', split_axis=1, concat_axis...  42.2 us
    reshape x2, local copies, waits for them, and re-layouts, shards(): packed.reshape(row_count, col_count, local_experts, capacity, 2 * model_w...  21.8 us
    dot_general x1, matrix products, shards(): jnp.einsum('emd,edf->emf', input_rows, w_gate_up, preferred_element_type=...  19.6 us
    dot_general x1, matrix products, shards(): jnp.einsum('emf,edf->emd', pre_grad, w_gate_up, preferred_element_type=jn...  18.3 us
    another operation x2, local copies, waits for them, and re-layouts, shards(): part_back.reshape(row_count, col_count, local_experts, capacity, model_wi...  14.4 us
  transfers between devices with their start and end apart: 4, of which 2 were waited for; matrix products, arithmetic and copies ran while one was open for 10% of the time, Pallas kernels for 0%

commit v1 on v0

v1 whole, which is shorter than its diff:
```python
import functools

import jax
import jax.numpy as jnp
from jax import lax
from jax.experimental import pallas as pl
from jax.experimental.pallas import tpu as pltpu
from jax.sharding import PartitionSpec as P

MESH = pl.DeviceIdType.MESH
BF = jnp.bfloat16
F32 = jnp.float32

swish_alpha = 1.702

DEVICES = 128
TOK = 128
ROUTES = 4
WIDTH = 2880
UNITS = 1440
WIRE = 1920
BACK = 1024
CHUNKS = 4
PER = DEVICES // CHUNKS
ROWS = PER * 16
GROUPS = PER // 16
M = PER * 5
WIDE = 1536


def dot(a, b):
    return jnp.dot(a, b, preferred_element_type=F32)


def dot_nt(a, b):
    return lax.dot_general(a, b, (((1,), (1,)), ((), ())), preferred_element_type=F32)


def iota(shape, axis):
    return lax.broadcasted_iota(jnp.int32, shape, axis)


def peer(place, sign):
    row, col = lax.axis_index("row"), lax.axis_index("col")
    step = place % 64
    a, b, c = step % 4, (step // 4) % 4, step // 16
    dx, dy, dz, dc = a, (a + b) % 4, (a + c) % 4, place // 64
    x = (row // 4 + sign * dx + 4) % 4
    y = (row % 4 + sign * dy + 4) % 4
    z = (col // 2 + sign * dz + 4) % 4
    core = (col % 2 + dc) % 2
    return (x * 4 + y, z * 2 + core)


def places_of(experts):
    row, col = lax.axis_index("row"), lax.axis_index("col")
    dx = ((experts >> 5) - row // 4) & 3
    dy = ((experts >> 3) - row % 4) & 3
    dz = ((experts >> 1) - col // 2) & 3
    dc = (experts - col % 2) & 1
    return dc * 64 + ((dz - dx) & 3) * 16 + ((dy - dx) & 3) * 4 + dx


def wire_row(r):
    q = r & 15
    part = (q * 13) >> 6
    return part, q - 5 * part + 1


def kernel(
    ids_ref, gates_ref, grad_ref, tok_ref, wgu_hbm, wd_hbm,
    out_ref, route_ref,
    wgu, wd, xs, slot_tp, gate_tp, sbuf, rbuf, psend, precv, gl, tl, proj, hg, pg, pst, acc, racc,
    wsem, ssem, rsem, pssem, prsem,
):
    load_gu = pltpu.make_async_copy(wgu_hbm.at[0], wgu, wsem.at[0])
    load_d = pltpu.make_async_copy(wd_hbm.at[0], wd, wsem.at[1])
    load_gu.start()
    load_d.start()

    barrier = pltpu.get_barrier_semaphore()

    @pl.loop(1, DEVICES)
    def _(p):
        pl.semaphore_signal(barrier, inc=1, device_id=peer(p, 1), device_id_type=MESH)

    places = places_of(ids_ref[...])
    lanes = iota((TOK, DEVICES), 1)
    chosen = jnp.zeros((TOK, DEVICES), F32)
    weight = jnp.zeros((TOK, DEVICES), F32)
    for k in range(ROUTES):
        hit = places[:, k : k + 1] == lanes
        chosen = jnp.where(hit, 1.0, chosen)
        weight = jnp.where(hit, gates_ref[:, k : k + 1], weight)
    earlier = (iota((TOK, TOK), 1) < iota((TOK, TOK), 0)).astype(F32).astype(BF)
    taken = dot(earlier, chosen.astype(BF))
    slot_tp[...] = (chosen * (taken + 1.0)).astype(BF)
    gate_tp[...] = weight.astype(BF)

    xs[0:128, :] = grad_ref[:, 0:1920]
    xs[128:256, :] = tok_ref[:, 0:1920]
    xs[256:384, 0:896] = grad_ref[:, 1920:2816]
    xs[256:384, 896:1792] = tok_ref[:, 1920:2816]
    low = (iota((64, 128), 0) == iota((64, 128), 1)).astype(F32).astype(BF)
    high = (iota((64, 128), 0) + 64 == iota((64, 128), 1)).astype(F32).astype(BF)
    xs[256:384, 1792:1920] = (
        dot(grad_ref[:, 2816:2880], low) + dot(tok_ref[:, 2816:2880], high)
    ).astype(BF)

    def pack(c):
        for g in range(ROWS // 256):
            base = c * ROWS + g * 256
            r = iota((256, 128), 0)
            spread = (iota((256, 128), 1) == c * PER + g * 16 + (r >> 4)).astype(F32).astype(BF)
            slots = dot_nt(spread, slot_tp[...])
            part, slot = wire_row(r)
            match = slots == slot.astype(F32)
            pick = jnp.concatenate(
                [jnp.where(match & (part == j), 1.0, 0.0).astype(BF) for j in range(3)], axis=1
            )

            @pl.loop(0, 5)
            def _(n):
                cols = pl.ds(pl.multiple_of(n * 384, 128), 384)
                sbuf[pl.ds(pl.multiple_of(base, 256), 256), cols] = dot(pick, xs[:, cols]).astype(BF)

    def forward(p, c):
        rows = pl.ds(pl.multiple_of(p * 16, 16), 16)
        return pltpu.make_async_remote_copy(
            src_ref=sbuf.at[rows], dst_ref=rbuf.at[rows],
            send_sem=ssem.at[c], recv_sem=rsem.at[c],
            device_id=peer(p, 1), device_id_type=MESH,
        )

    def backward(p, c):
        rows = pl.ds(pl.multiple_of(p * 16, 16), 16)
        return pltpu.make_async_remote_copy(
            src_ref=psend.at[rows], dst_ref=precv.at[rows],
            send_sem=pssem.at[c], recv_sem=prsem.at[c],
            device_id=peer(p, -1), device_id_type=MESH,
        )

    pack(0)
    pl.semaphore_wait(barrier, DEVICES - 1)
    pltpu.make_async_copy(sbuf.at[0:16], rbuf.at[0:16], rsem.at[0]).start()

    @pl.loop(1, PER)
    def _(p):
        forward(p, 0).start()

    @pl.loop(1, CHUNKS)
    def _(c):
        pack(c)

        @pl.loop(0, PER)
        def _(i):
            forward(c * PER + i, c).start()

    pst[...] = jnp.zeros_like(pst)
    acc[...] = jnp.zeros_like(acc)
    racc[...] = jnp.zeros_like(racc)
    load_gu.wait()
    load_d.wait()

    def chunk_rows(c):
        return pl.ds(pl.multiple_of(c * ROWS, 16), ROWS)

    @pl.loop(0, CHUNKS)
    def _(c):
        rows = chunk_rows(c)
        pltpu.make_async_copy(sbuf.at[rows], rbuf.at[rows], rsem.at[c]).wait()

        part, slot = wire_row(iota((240, 256), 1))
        target = part * 80 + (iota((240, 256), 1) >> 4) * 5 + slot - 1
        sort = ((target == iota((240, 256), 0)) & (part < 3)).astype(F32).astype(BF)
        down = (iota((128, 128), 0) == iota((128, 128), 1) + 64).astype(F32).astype(BF)
        for g in range(GROUPS):
            src = pl.ds(pl.multiple_of(c * ROWS + g * 256, 256), 256)
            dst = slice(g * 80, g * 80 + 80)
            for n0, n1 in ((0, 256), (256, 512), (512, 896), (896, 1152), (1152, 1408), (1408, 1792), (1792, 1920)):
                got = dot(sort, rbuf[src, n0:n1]).astype(BF)
                gl[dst, n0:n1] = got[0:80]
                tl[dst, n0:n1] = got[80:160]
                if n1 <= 896:
                    gl[dst, 1920 + n0 : 1920 + n1] = got[160:240]
                elif n1 <= 1792:
                    tl[dst, 1024 + n0 : 1024 + n1] = got[160:240]
                else:
                    gl[dst, 2816:2880] = got[160:240, 0:64]
                    tl[dst, 2816:2880] = dot(got[160:240], down).astype(BF)[:, 0:64]

        @pl.loop(0, 11)
        def _(n):
            cols = pl.ds(pl.multiple_of(n * 256, 256), 256)
            proj[:, cols] = dot(tl[...], wgu[:, cols])

        proj[:, 2816:2880] = dot(tl[...], wgu[:, 2816:2880])

        @pl.loop(0, 5)
        def _(n):
            at = pl.ds(pl.multiple_of(n * 256, 256), 256)
            hg[:, at] = dot_nt(gl[...], wd[at, :])

        hg[:, 1280:1440] = dot_nt(gl[...], wd[1280:1440, :])

        @pl.loop(0, M // 16)
        def _(b):
            at = pl.ds(pl.multiple_of(b * 16, 16), 16)
            real = iota((16, WIDE), 1) < UNITS
            gate = proj[at, 0:WIDE]
            up1 = jnp.where(real, pltpu.roll(proj[at, 1408:2944], WIDE - 32, 1), 0.0) + 1.0
            hidden_grad = jnp.where(real, hg[at, :], 0.0)
            sig = 1.0 / (1.0 + jnp.exp(-swish_alpha * gate))
            act = gate * sig
            up_grad = hidden_grad * act
            term = jnp.sum(up_grad * up1, axis=1, keepdims=True)
            gate_grad = hidden_grad * up1 * sig * (1.0 + swish_alpha * gate * (1.0 - sig))
            moved = pltpu.roll(up_grad, 32, 1)
            pg[at, 0:1408] = gate_grad[:, 0:1408].astype(BF)
            pg[at, 1408:1536] = (gate_grad[:, 1408:1536] + moved[:, 0:128]).astype(BF)
            pg[at, 1536:2944] = moved[:, 128:1536].astype(BF)
            coarse = term.astype(BF).astype(F32)
            tile = iota((16, 128), 1)
            pair = jnp.where(tile == 0, coarse, jnp.where(tile == 1, term - coarse, 0.0)).astype(BF)
            group = b // 5
            pst[pl.ds(pl.multiple_of(group * 240 + 160 + (b - group * 5) * 16, 16), 16), 896:1024] = pair

        def put(part_of, lane, cols, value):
            value = value.astype(BF)
            for g in range(GROUPS):
                at = pl.ds(pl.multiple_of(g * 240 + part_of * 80, 16), 80)
                if cols == 64:
                    pst[at, 768:832] = value[g * 80 : g * 80 + 80]
                else:
                    pst[at, pl.ds(pl.multiple_of(lane, 256), cols)] = value[g * 80 : g * 80 + 80]

        @pl.loop(0, 11)
        def _(n):
            at = pl.ds(pl.multiple_of(n * 256, 256), 256)
            put(n // 4, (n % 4) * 256, 256, dot_nt(pg[:, 0:WIDTH], wgu[at, :]))

        put(2, 768, 64, dot_nt(pg[:, 0:WIDTH], wgu[2816:2880, :]))

        part, slot = wire_row(iota((256, 240), 0))
        target = part * 80 + (iota((256, 240), 0) >> 4) * 5 + slot - 1
        unsort = ((target == iota((256, 240), 1)) & (part < 3)).astype(F32).astype(BF)
        for g in range(GROUPS):
            dst = pl.ds(pl.multiple_of(c * ROWS + g * 256, 256), 256)
            for n in range(4):
                psend[dst, n * 256 : n * 256 + 256] = dot(
                    unsort, pst[g * 240 : g * 240 + 240, n * 256 : n * 256 + 256]
                ).astype(BF)

        @pl.when(c == 0)
        def _():
            pltpu.make_async_copy(psend.at[0:16], precv.at[0:16], prsem.at[0]).start()

        @pl.loop(jnp.where(c == 0, 1, 0), PER)
        def _(i):
            backward(c * PER + i, c).start()

    places_home = places_of(ids_ref[...])

    @pl.loop(0, CHUNKS)
    def _(c):
        rows = chunk_rows(c)
        pltpu.make_async_copy(psend.at[rows], precv.at[rows], prsem.at[c]).wait()
        place_of = c * PER + (iota((128, ROWS), 1) >> 4)
        spread = (iota((128, ROWS), 0) == place_of).astype(F32).astype(BF)
        slots = dot(slot_tp[...], spread)
        weights = dot(gate_tp[...], spread)
        part, slot = wire_row(iota((128, ROWS), 1))
        match = slots == slot.astype(F32)
        mix = jnp.concatenate(
            [jnp.where(match & (part == j), weights, 0.0).astype(BF) for j in range(3)], axis=0
        )
        for n in range(4):
            acc[:, n * 256 : n * 256 + 256] += dot(mix, precv[rows, n * 256 : n * 256 + 256])
        last = match & (part == 2)
        find = jnp.concatenate(
            [
                jnp.where(last & (places_home[:, k : k + 1] == place_of), 1.0, 0.0).astype(BF)
                for k in range(ROUTES)
            ],
            axis=0,
        )
        racc[...] += dot(find, precv[rows, 896:1024])

    out_ref[:, 0:1024] = acc[0:128, :].astype(BF)
    out_ref[:, 1024:2048] = acc[128:256, :].astype(BF)
    out_ref[:, 2048:2880] = acc[256:384, 0:832].astype(BF)
    terms = jnp.zeros((TOK, 128), F32)
    for k in range(ROUTES):
        found = racc[k * 128 : k * 128 + 128, :]
        terms = jnp.where(lanes == k, found[:, 0:1] + found[:, 1:2], terms)
    route_ref[...] = terms[:, 0:ROUTES]

    for c in range(CHUNKS):
        rows = pl.ds(16 if c == 0 else c * ROWS, ROWS - 16 if c == 0 else ROWS)
        pltpu.make_async_copy(sbuf.at[rows], rbuf.at[rows], ssem.at[c]).wait()
        pltpu.make_async_copy(psend.at[rows], precv.at[rows], pssem.at[c]).wait()


def shards(out_grad, tokens, expert_ids, gates, w_gate_up, w_down):
    vmem = pl.BlockSpec(memory_space=pltpu.VMEM)
    hbm = pl.BlockSpec(memory_space=pl.ANY)
    return pl.pallas_call(
        kernel,
        out_shape=(
            jax.ShapeDtypeStruct((TOK, WIDTH), BF),
            jax.ShapeDtypeStruct((TOK, ROUTES), F32),
        ),
        in_specs=[vmem, vmem, vmem, vmem, hbm, hbm],
        out_specs=(vmem, vmem),
        scratch_shapes=[
            pltpu.VMEM((WIDTH, WIDTH), BF),
            pltpu.VMEM((UNITS, WIDTH), BF),
            pltpu.VMEM((384, WIRE), BF),
            pltpu.VMEM((TOK, DEVICES), BF),
            pltpu.VMEM((TOK, DEVICES), BF),
            pltpu.VMEM((DEVICES * 16, WIRE), BF),
            pltpu.VMEM((DEVICES * 16, WIRE), BF),
            pltpu.VMEM((DEVICES * 16, BACK), BF),
            pltpu.VMEM((DEVICES * 16, BACK), BF),
            pltpu.VMEM((M, WIDTH), BF),
            pltpu.VMEM((M, WIDTH), BF),
            pltpu.VMEM((M, 2944), F32),
            pltpu.VMEM((M, WIDE), F32),
            pltpu.VMEM((M, 2944), BF),
            pltpu.VMEM((GROUPS * 240, BACK), BF),
            pltpu.VMEM((384, BACK), F32),
            pltpu.VMEM((ROUTES * TOK, 128), F32),
            pltpu.SemaphoreType.DMA((2,)),
            pltpu.SemaphoreType.DMA((CHUNKS,)),
            pltpu.SemaphoreType.DMA((CHUNKS,)),
            pltpu.SemaphoreType.DMA((CHUNKS,)),
            pltpu.SemaphoreType.DMA((CHUNKS,)),
        ],
        compiler_params=pltpu.CompilerParams(
            collective_id=0, has_side_effects=True, vmem_limit_bytes=63 * 2**20
        ),
    )(expert_ids, gates, out_grad, tokens, w_gate_up, w_down)


def solution(mesh):
    rows = P(("row", "col"), None)
    blocks = P(("row", "col"), None, None)
    return jax.shard_map(
        shards,
        mesh=mesh,
        in_specs=(rows, rows, rows, rows, blocks, blocks),
        out_specs=(rows, rows),
        check_vma=False,
    )
```

time: 467 us -> 195 us (0.42)
  the two profiles are of different devices: /device:TPU:5 before, /device:TPU:83 now
where the time goes in v1:
time: 195 us; the launch traced here: 194 us
  Pallas kernels  183 us (94%)
  local copies, waits for them, and re-layouts  11.1 us (6%)
    pallas_call x1, Pallas kernels, shards(): pl.pallas_call(kernel, out_shape=(jax.ShapeDtypeStruct((TOK, WIDTH), BF),...  183 us
    unnamed x4, local copies, waits for them, and re-layouts  7.37 us

profile of v1, /device:TPU:83, one launch (start us, length us, event | category | flops | bytes accessed | tf_op | source)
XLA Modules:
  0.0 194.3 jit_solution(15777326967177639853)
XLA Ops:
  0.6 1.4 copy.8.ids_ref
  2.0 1.4 copy.9.gates_ref
  3.5 2.3 %copy.10.grad_ref = bf16[128,2880]{1,0:T(8,128)(2,1)} copy(bf16[128,2880]{0,1:T(8,128)(2,1)} %param.6) | data formatting | bytes 1474560 | tf_op args[0]
  5.7 2.3 %copy.11.tok_ref = bf16[128,2880]{1,0:T(8,128)(2,1)} copy(bf16[128,2880]{0,1:T(8,128)(2,1)} %param.7) | data formatting | bytes 1474560 | tf_op args[1]
  8.0 182.5 %shard_map.77 = (bf16[128,2880]{1,0:T(8,128)(2,1)}, f32[128,4]{1,0:T(8,128)}) custom-call(s32[128,4]{1,0:T(8,128)} %copy.8.ids_ref, f32[128,4]{1,0:T(8,128)} %copy.9.gates_ref, bf16[128,2880]{1,0:T(8,128)(2,1)} %copy.10.grad_ref, bf16[128,2880]{1,0:T(8,128)(2,1)} %copy.11.tok_ref, bf16[1,2880,2880]{2,1,0:T(8,128)(2,1)} %wgu_hbm.1, bf16[1,1440,2880]{2,1,0:T(8,128)(2,1)} %wd_hbm.1), custom_call_target="tpu_custom_call" | custom-call | tf_op jit(solution)/shard_map/pallas_call | solution.py:307
  190.5 2.3 %copy.12 = bf16[128,2880]{0,1:T(8,128)(2,1)} copy(bf16[128,2880]{1,0:T(8,128)(2,1)} %get-tuple-element.2) | data formatting | bytes 1474560 | tf_op jit(solution)/shard_map/pallas_call | solution.py:307
  192.8 1.5 copy.13

commit v2 on v1

--- a/solution.py
+++ b/solution.py
@@ -42,14 +42,17 @@
 
 def peer(place, sign):
     row, col = lax.axis_index("row"), lax.axis_index("col")
-    step = place % 64
-    a, b, c = step % 4, (step // 4) % 4, step // 16
-    dx, dy, dz, dc = a, (a + b) % 4, (a + c) % 4, place // 64
-    x = (row // 4 + sign * dx + 4) % 4
-    y = (row % 4 + sign * dy + 4) % 4
-    z = (col // 2 + sign * dz + 4) % 4
-    core = (col % 2 + dc) % 2
+    step = place & 63
+    a, b, c = step & 3, (step >> 2) & 3, step >> 4
+    x = ((row >> 2) + sign * a) & 3
+    y = ((row & 3) + sign * (a + b)) & 3
+    z = ((col >> 1) + sign * (a + c)) & 3
+    core = (col + (place >> 6)) & 1
     return (x * 4 + y, z * 2 + core)
+
+
+def turn(i):
+    return jnp.where(lax.axis_index("col") % 2 == 1, PER - 1 - i, i)
 
 
 def places_of(experts):
@@ -70,7 +73,7 @@
 def kernel(
     ids_ref, gates_ref, grad_ref, tok_ref, wgu_hbm, wd_hbm,
     out_ref, route_ref,
-    wgu, wd, xs, slot_tp, gate_tp, sbuf, rbuf, psend, precv, gl, tl, proj, hg, pg, pst, acc, racc,
+    wgu, wd, xs, slot_pt, slot_tp, gate_tp, sbuf, rbuf, psend, precv, gl, tl, proj, hg, pg, pst, acc, terms,
     wsem, ssem, rsem, pssem, prsem,
 ):
     load_gu = pltpu.make_async_copy(wgu_hbm.at[0], wgu, wsem.at[0])
@@ -80,39 +83,44 @@
 
     barrier = pltpu.get_barrier_semaphore()
 
-    @pl.loop(1, DEVICES)
-    def _(p):
-        pl.semaphore_signal(barrier, inc=1, device_id=peer(p, 1), device_id_type=MESH)
+    row, col = lax.axis_index("row"), lax.axis_index("col")
+    for p in range(1, DEVICES):
+        x, y = ((row >> 2) + (p >> 5)) & 3, ((row & 3) + (p >> 3)) & 3
+        z, core = ((col >> 1) + (p >> 1)) & 3, (col + p) & 1
+        pl.semaphore_signal(
+            barrier, inc=1, device_id=(x * 4 + y, z * 2 + core), device_id_type=MESH
+        )
 
     places = places_of(ids_ref[...])
-    lanes = iota((TOK, DEVICES), 1)
-    chosen = jnp.zeros((TOK, DEVICES), F32)
-    weight = jnp.zeros((TOK, DEVICES), F32)
+    down = iota((DEVICES, TOK), 0)
+    hits = [places[k : k + 1, :] == down for k in range(ROUTES)]
+    chosen = jnp.zeros((DEVICES, TOK), F32)
+    weight = jnp.zeros((DEVICES, TOK), F32)
     for k in range(ROUTES):
-        hit = places[:, k : k + 1] == lanes
-        chosen = jnp.where(hit, 1.0, chosen)
-        weight = jnp.where(hit, gates_ref[:, k : k + 1], weight)
-    earlier = (iota((TOK, TOK), 1) < iota((TOK, TOK), 0)).astype(F32).astype(BF)
-    taken = dot(earlier, chosen.astype(BF))
-    slot_tp[...] = (chosen * (taken + 1.0)).astype(BF)
-    gate_tp[...] = weight.astype(BF)
-
-    xs[0:128, :] = grad_ref[:, 0:1920]
-    xs[128:256, :] = tok_ref[:, 0:1920]
-    xs[256:384, 0:896] = grad_ref[:, 1920:2816]
-    xs[256:384, 896:1792] = tok_ref[:, 1920:2816]
-    low = (iota((64, 128), 0) == iota((64, 128), 1)).astype(F32).astype(BF)
-    high = (iota((64, 128), 0) + 64 == iota((64, 128), 1)).astype(F32).astype(BF)
-    xs[256:384, 1792:1920] = (
-        dot(grad_ref[:, 2816:2880], low) + dot(tok_ref[:, 2816:2880], high)
-    ).astype(BF)
+        chosen = jnp.where(hits[k], 1.0, chosen)
+        weight = jnp.where(hits[k], gates_ref[k : k + 1, :], weight)
+    earlier = (iota((TOK, TOK), 0) < iota((TOK, TOK), 1)).astype(F32).astype(BF)
+    same = (iota((TOK, TOK), 0) == iota((TOK, TOK), 1)).astype(F32).astype(BF)
+    slot_pt[...] = (chosen * (dot(chosen.astype(BF), earlier) + 1.0)).astype(BF)
+    slot_tp[...] = dot_nt(same, slot_pt[...]).astype(BF)
+    gate_tp[...] = dot_nt(same, weight.astype(BF)).astype(BF)
+
+    for n in range(0, 1920, 384):
+        xs[0:128, n : n + 384] = dot_nt(same, grad_ref[n : n + 384, :]).astype(BF)
+        xs[128:256, n : n + 384] = dot_nt(same, tok_ref[n : n + 384, :]).astype(BF)
+    for n, size in ((0, 384), (384, 512)):
+        at = slice(1920 + n, 1920 + n + size)
+        xs[256:384, n : n + size] = dot_nt(same, grad_ref[at, :]).astype(BF)
+        xs[256:384, 896 + n : 896 + n + size] = dot_nt(same, tok_ref[at, :]).astype(BF)
+    ends = jnp.concatenate([grad_ref[2816:2880, :], tok_ref[2816:2880, :]], axis=0)
+    xs[256:384, 1792:1920] = dot_nt(same, ends).astype(BF)
 
     def pack(c):
         for g in range(ROWS // 256):
             base = c * ROWS + g * 256
             r = iota((256, 128), 0)
             spread = (iota((256, 128), 1) == c * PER + g * 16 + (r >> 4)).astype(F32).astype(BF)
-            slots = dot_nt(spread, slot_tp[...])
+            slots = dot(spread, slot_pt[...])
             part, slot = wire_row(r)
             match = slots == slot.astype(F32)
             pick = jnp.concatenate(
@@ -144,9 +152,13 @@
     pl.semaphore_wait(barrier, DEVICES - 1)
     pltpu.make_async_copy(sbuf.at[0:16], rbuf.at[0:16], rsem.at[0]).start()
 
-    @pl.loop(1, PER)
-    def _(p):
-        forward(p, 0).start()
+    @pl.loop(0, PER)
+    def _(i):
+        p = turn(i)
+
+        @pl.when(p != 0)
+        def _():
+            forward(p, 0).start()
 
     @pl.loop(1, CHUNKS)
     def _(c):
@@ -154,11 +166,10 @@
 
         @pl.loop(0, PER)
         def _(i):
-            forward(c * PER + i, c).start()
+            forward(c * PER + turn(i), c).start()
 
     pst[...] = jnp.zeros_like(pst)
     acc[...] = jnp.zeros_like(acc)
-    racc[...] = jnp.zeros_like(racc)
     load_gu.wait()
     load_d.wait()
 
@@ -173,7 +184,7 @@
         part, slot = wire_row(iota((240, 256), 1))
         target = part * 80 + (iota((240, 256), 1) >> 4) * 5 + slot - 1
         sort = ((target == iota((240, 256), 0)) & (part < 3)).astype(F32).astype(BF)
-        down = (iota((128, 128), 0) == iota((128, 128), 1) + 64).astype(F32).astype(BF)
+        shift = (iota((128, 128), 0) == iota((128, 128), 1) + 64).astype(F32).astype(BF)
         for g in range(GROUPS):
             src = pl.ds(pl.multiple_of(c * ROWS + g * 256, 256), 256)
             dst = slice(g * 80, g * 80 + 80)
@@ -187,7 +198,7 @@
                     tl[dst, 1024 + n0 : 1024 + n1] = got[160:240]
                 else:
                     gl[dst, 2816:2880] = got[160:240, 0:64]
-                    tl[dst, 2816:2880] = dot(got[160:240], down).astype(BF)[:, 0:64]
+                    tl[dst, 2816:2880] = dot(got[160:240], shift).astype(BF)[:, 0:64]
 
         @pl.loop(0, 11)
         def _(n):
@@ -255,11 +266,13 @@
         def _():
             pltpu.make_async_copy(psend.at[0:16], precv.at[0:16], prsem.at[0]).start()
 
-        @pl.loop(jnp.where(c == 0, 1, 0), PER)
+        @pl.loop(0, PER)
         def _(i):
-            backward(c * PER + i, c).start()
-
-    places_home = places_of(ids_ref[...])
+            p = c * PER + turn(i)
+
+            @pl.when(p != 0)
+            def _():
+                backward(p, c).start()
 
     @pl.loop(0, CHUNKS)
     def _(c):
@@ -276,24 +289,23 @@
         )
         for n in range(4):
             acc[:, n * 256 : n * 256 + 256] += dot(mix, precv[rows, n * 256 : n * 256 + 256])
-        last = match & (part == 2)
-        find = jnp.concatenate(
-            [
-                jnp.where(last & (places_home[:, k : k + 1] == place_of), 1.0, 0.0).astype(BF)
-                for k in range(ROUTES)
-            ],
-            axis=0,
-        )
-        racc[...] += dot(find, precv[rows, 896:1024])
+        out, at = iota((5 * PER, ROWS), 0), iota((5 * PER, ROWS), 1)
+        number = out // PER
+        find = ((out - number * PER) == (at >> 4)) & ((at & 15) == number + 10)
+        found = dot(find.astype(F32).astype(BF), precv[rows, 896:1024])
+        for i in range(5):
+            terms[i, pl.ds(pl.multiple_of(c * PER, 16), PER), :] = found[i * PER : i * PER + PER]
 
     out_ref[:, 0:1024] = acc[0:128, :].astype(BF)
     out_ref[:, 1024:2048] = acc[128:256, :].astype(BF)
     out_ref[:, 2048:2880] = acc[256:384, 0:832].astype(BF)
-    terms = jnp.zeros((TOK, 128), F32)
+    taken = slot_pt[...].astype(F32)
+    value = jnp.zeros((DEVICES, TOK), F32)
+    for i in range(5):
+        value = jnp.where(taken == i + 1, terms[i, :, 0:1] + terms[i, :, 1:2], value)
     for k in range(ROUTES):
-        found = racc[k * 128 : k * 128 + 128, :]
-        terms = jnp.where(lanes == k, found[:, 0:1] + found[:, 1:2], terms)
-    route_ref[...] = terms[:, 0:ROUTES]
+        hit = places[k : k + 1, :] == down
+        route_ref[k : k + 1, :] = jnp.sum(jnp.where(hit, value, 0.0), axis=0, keepdims=True)
 
     for c in range(CHUNKS):
         rows = pl.ds(16 if c == 0 else c * ROWS, ROWS - 16 if c == 0 else ROWS)
@@ -304,11 +316,11 @@
 def shards(out_grad, tokens, expert_ids, gates, w_gate_up, w_down):
     vmem = pl.BlockSpec(memory_space=pltpu.VMEM)
     hbm = pl.BlockSpec(memory_space=pl.ANY)
-    return pl.pallas_call(
+    input_grad, route_grad = pl.pallas_call(
         kernel,
         out_shape=(
             jax.ShapeDtypeStruct((TOK, WIDTH), BF),
-            jax.ShapeDtypeStruct((TOK, ROUTES), F32),
+            jax.ShapeDtypeStruct((ROUTES, TOK), F32),
         ),
         in_specs=[vmem, vmem, vmem, vmem, hbm, hbm],
         out_specs=(vmem, vmem),
@@ -316,6 +328,7 @@
             pltpu.VMEM((WIDTH, WIDTH), BF),
             pltpu.VMEM((UNITS, WIDTH), BF),
             pltpu.VMEM((384, WIRE), BF),
+            pltpu.VMEM((DEVICES, TOK), BF),
             pltpu.VMEM((TOK, DEVICES), BF),
             pltpu.VMEM((TOK, DEVICES), BF),
             pltpu.VMEM((DEVICES * 16, WIRE), BF),
@@ -329,7 +342,7 @@
             pltpu.VMEM((M, 2944), BF),
             pltpu.VMEM((GROUPS * 240, BACK), BF),
             pltpu.VMEM((384, BACK), F32),
-            pltpu.VMEM((ROUTES * TOK, 128), F32),
+            pltpu.VMEM((5, DEVICES, 128), F32),
             pltpu.SemaphoreType.DMA((2,)),
             pltpu.SemaphoreType.DMA((CHUNKS,)),
             pltpu.SemaphoreType.DMA((CHUNKS,)),
@@ -339,7 +352,8 @@
         compiler_params=pltpu.CompilerParams(
             collective_id=0, has_side_effects=True, vmem_limit_bytes=63 * 2**20
         ),
-    )(expert_ids, gates, out_grad, tokens, w_gate_up, w_down)
+    )(expert_ids.T, gates.T, out_grad.T, tokens.T, w_gate_up, w_down)
+    return input_grad, route_grad.T
 
 
 def solution(mesh):

time: 195 us -> 171 us (0.88)
  the two profiles are of different devices: /device:TPU:83 before, /device:TPU:5 now
where the time goes in v2:
time: 171 us; the launch traced here: 170 us
  Pallas kernels  166 us (97%)
  local copies, waits for them, and re-layouts  3.51 us (2%)
    pallas_call x1, Pallas kernels, shards(): pl.pallas_call(kernel, out_shape=(jax.ShapeDtypeStruct((TOK, WIDTH), BF),...  166 us
    unnamed x2, local copies, waits for them, and re-layouts  3.51 us

profile of v2, /device:TPU:5, one launch (start us, length us, event | category | flops | bytes accessed | tf_op | source)
XLA Modules:
  0.0 170.5 jit_solution(15097860302533314133)
XLA Ops:
  0.6 166.3 %shard_map.77 = (bf16[128,2880]{1,0:T(8,128)(2,1)}, f32[4,128]{1,0:T(4,128)}) custom-call(s32[4,128]{1,0:T(4,128)} %bitcast.8, f32[4,128]{1,0:T(4,128)} %bitcast.9, bf16[2880,128]{1,0:T(8,128)(2,1)} %bitcast.5, bf16[2880,128]{1,0:T(8,128)(2,1)} %bitcast.6, bf16[1,2880,2880]{2,1,0:T(8,128)(2,1)} %wgu_hbm.1, bf16[1,1440,2880]{2,1,0:T(8,128)(2,1)} %wd_hbm.1), custom_call_target="tpu_custom_call" | custom-call | tf_op jit(solution)/shard_map/pallas_call | solution.py:319
  167.0 2.3 %copy.8 = bf16[128,2880]{0,1:T(8,128)(2,1)} copy(bf16[128,2880]{1,0:T(8,128)(2,1)} %get-tuple-element.6) | data formatting | bytes 1474560
  169.2 1.3 copy.10

commit v3 on v2

--- a/solution.py
+++ b/solution.py
@@ -200,19 +200,19 @@
                     gl[dst, 2816:2880] = got[160:240, 0:64]
                     tl[dst, 2816:2880] = dot(got[160:240], shift).astype(BF)[:, 0:64]
 
-        @pl.loop(0, 11)
-        def _(n):
-            cols = pl.ds(pl.multiple_of(n * 256, 256), 256)
-            proj[:, cols] = dot(tl[...], wgu[:, cols])
-
-        proj[:, 2816:2880] = dot(tl[...], wgu[:, 2816:2880])
-
         @pl.loop(0, 5)
         def _(n):
-            at = pl.ds(pl.multiple_of(n * 256, 256), 256)
+            cols = pl.ds(pl.multiple_of(n * 512, 512), 512)
+            proj[:, cols] = dot(tl[...], wgu[:, cols])
+
+        proj[:, 2560:2880] = dot(tl[...], wgu[:, 2560:2880])
+
+        @pl.loop(0, 2)
+        def _(n):
+            at = pl.ds(pl.multiple_of(n * 512, 512), 512)
             hg[:, at] = dot_nt(gl[...], wd[at, :])
 
-        hg[:, 1280:1440] = dot_nt(gl[...], wd[1280:1440, :])
+        hg[:, 1024:1440] = dot_nt(gl[...], wd[1024:1440, :])
 
         @pl.loop(0, M // 16)
         def _(b):
@@ -240,17 +240,17 @@
             value = value.astype(BF)
             for g in range(GROUPS):
                 at = pl.ds(pl.multiple_of(g * 240 + part_of * 80, 16), 80)
-                if cols == 64:
-                    pst[at, 768:832] = value[g * 80 : g * 80 + 80]
+                if cols == 320:
+                    pst[at, 512:832] = value[g * 80 : g * 80 + 80]
                 else:
-                    pst[at, pl.ds(pl.multiple_of(lane, 256), cols)] = value[g * 80 : g * 80 + 80]
-
-        @pl.loop(0, 11)
+                    pst[at, pl.ds(pl.multiple_of(lane, 512), cols)] = value[g * 80 : g * 80 + 80]
+
+        @pl.loop(0, 5)
         def _(n):
-            at = pl.ds(pl.multiple_of(n * 256, 256), 256)
-            put(n // 4, (n % 4) * 256, 256, dot_nt(pg[:, 0:WIDTH], wgu[at, :]))
-
-        put(2, 768, 64, dot_nt(pg[:, 0:WIDTH], wgu[2816:2880, :]))
+            at = pl.ds(pl.multiple_of(n * 512, 512), 512)
+            put(n // 2, (n % 2) * 512, 512, dot_nt(pg[:, 0:WIDTH], wgu[at, :]))
+
+        put(2, 512, 320, dot_nt(pg[:, 0:WIDTH], wgu[2560:2880, :]))
 
         part, slot = wire_row(iota((256, 240), 0))
         target = part * 80 + (iota((256, 240), 0) >> 4) * 5 + slot - 1

time: 171 us -> 170 us (level)
  no operation moved by 1% of the time
where the time goes in v3:
time: 170 us
  Pallas kernels  166 us (98%)
  local copies, waits for them, and re-layouts  3.51 us (2%)
    pallas_call x1, Pallas kernels, shards(): pl.pallas_call(kernel, out_shape=(jax.ShapeDtypeStruct((TOK, WIDTH), BF),...  166 us
    unnamed x2, local copies, waits for them, and re-layouts  3.51 us

profile of v3, /device:TPU:5, one launch (start us, length us, event | category | flops | bytes accessed | tf_op | source)
XLA Modules:
  0.0 169.9 jit_solution(11171456326011946368)
XLA Ops:
  0.6 165.8 %shard_map.77 = (bf16[128,2880]{1,0:T(8,128)(2,1)}, f32[4,128]{1,0:T(4,128)}) custom-call(s32[4,128]{1,0:T(4,128)} %bitcast.8, f32[4,128]{1,0:T(4,128)} %bitcast.9, bf16[2880,128]{1,0:T(8,128)(2,1)} %bitcast.5, bf16[2880,128]{1,0:T(8,128)(2,1)} %bitcast.6, bf16[1,2880,2880]{2,1,0:T(8,128)(2,1)} %wgu_hbm.1, bf16[1,1440,2880]{2,1,0:T(8,128)(2,1)} %wd_hbm.1), custom_call_target="tpu_custom_call" | custom-call | tf_op jit(solution)/shard_map/pallas_call | solution.py:319
  166.4 2.3 %copy.8 = bf16[128,2880]{0,1:T(8,128)(2,1)} copy(bf16[128,2880]{1,0:T(8,128)(2,1)} %get-tuple-element.6) | data formatting | bytes 1474560
  168.7 1.3 copy.10

commit v4 on v3

--- a/solution.py
+++ b/solution.py
@@ -140,10 +140,11 @@
             device_id=peer(p, 1), device_id_type=MESH,
         )
 
-    def backward(p, c):
+    def backward(p, c, half):
         rows = pl.ds(pl.multiple_of(p * 16, 16), 16)
+        cols = slice(half * 512, half * 512 + 512)
         return pltpu.make_async_remote_copy(
-            src_ref=psend.at[rows], dst_ref=precv.at[rows],
+            src_ref=psend.at[rows, cols], dst_ref=precv.at[rows, cols],
             send_sem=pssem.at[c], recv_sem=prsem.at[c],
             device_id=peer(p, -1), device_id_type=MESH,
         )
@@ -243,36 +244,39 @@
                 if cols == 320:
                     pst[at, 512:832] = value[g * 80 : g * 80 + 80]
                 else:
-                    pst[at, pl.ds(pl.multiple_of(lane, 512), cols)] = value[g * 80 : g * 80 + 80]
-
-        @pl.loop(0, 5)
-        def _(n):
-            at = pl.ds(pl.multiple_of(n * 512, 512), 512)
-            put(n // 2, (n % 2) * 512, 512, dot_nt(pg[:, 0:WIDTH], wgu[at, :]))
-
-        put(2, 512, 320, dot_nt(pg[:, 0:WIDTH], wgu[2560:2880, :]))
+                    pst[at, lane : lane + cols] = value[g * 80 : g * 80 + 80]
 
         part, slot = wire_row(iota((256, 240), 0))
         target = part * 80 + (iota((256, 240), 0) >> 4) * 5 + slot - 1
         unsort = ((target == iota((256, 240), 1)) & (part < 3)).astype(F32).astype(BF)
-        for g in range(GROUPS):
-            dst = pl.ds(pl.multiple_of(c * ROWS + g * 256, 256), 256)
-            for n in range(4):
-                psend[dst, n * 256 : n * 256 + 256] = dot(
-                    unsort, pst[g * 240 : g * 240 + 240, n * 256 : n * 256 + 256]
-                ).astype(BF)
+
+        for half in range(2):
+
+            @pl.loop(0, 3 - half)
+            def _(n):
+                at = pl.ds(pl.multiple_of(n * 1024 + half * 512, 512), 512)
+                put(n, half * 512, 512, dot_nt(pg[:, 0:WIDTH], wgu[at, :]))
+
+            if half == 1:
+                put(2, 512, 320, dot_nt(pg[:, 0:WIDTH], wgu[2560:2880, :]))
+            for g in range(GROUPS):
+                dst = pl.ds(pl.multiple_of(c * ROWS + g * 256, 256), 256)
+                for n in range(2 * half, 2 * half + 2):
+                    psend[dst, n * 256 : n * 256 + 256] = dot(
+                        unsort, pst[g * 240 : g * 240 + 240, n * 256 : n * 256 + 256]
+                    ).astype(BF)
+
+            @pl.loop(0, PER)
+            def _(i):
+                p = c * PER + turn(i)
+
+                @pl.when(p != 0)
+                def _():
+                    backward(p, c, half).start()
 
         @pl.when(c == 0)
         def _():
             pltpu.make_async_copy(psend.at[0:16], precv.at[0:16], prsem.at[0]).start()
-
-        @pl.loop(0, PER)
-        def _(i):
-            p = c * PER + turn(i)
-
-            @pl.when(p != 0)
-            def _():
-                backward(p, c).start()
 
     @pl.loop(0, CHUNKS)
     def _(c):

time: 170 us -> 174 us (1.024)
  the two profiles are of different devices: /device:TPU:5 before, /device:TPU:2 now
where the time goes in v4:
time: 174 us
  Pallas kernels  170 us (98%)
  local copies, waits for them, and re-layouts  3.51 us (2%)
    pallas_call x1, Pallas kernels, shards(): pl.pallas_call(kernel, out_shape=(jax.ShapeDtypeStruct((TOK, WIDTH), BF),...  170 us
    unnamed x2, local copies, waits for them, and re-layouts  3.51 us

profile of v4, /device:TPU:2, one launch (start us, length us, event | category | flops | bytes accessed | tf_op | source)
XLA Modules:
  0.0 174.3 jit_solution(9436322602211104088)
XLA Ops:
  0.6 170.1 %shard_map.77 = (bf16[128,2880]{1,0:T(8,128)(2,1)}, f32[4,128]{1,0:T(4,128)}) custom-call(s32[4,128]{1,0:T(4,128)} %bitcast.8, f32[4,128]{1,0:T(4,128)} %bitcast.9, bf16[2880,128]{1,0:T(8,128)(2,1)} %bitcast.5, bf16[2880,128]{1,0:T(8,128)(2,1)} %bitcast.6, bf16[1,2880,2880]{2,1,0:T(8,128)(2,1)} %wgu_hbm.1, bf16[1,1440,2880]{2,1,0:T(8,128)(2,1)} %wd_hbm.1), custom_call_target="tpu_custom_call" | custom-call | tf_op jit(solution)/shard_map/pallas_call | solution.py:323
  170.8 2.3 %copy.8 = bf16[128,2880]{0,1:T(8,128)(2,1)} copy(bf16[128,2880]{1,0:T(8,128)(2,1)} %get-tuple-element.6) | data formatting | bytes 1474560
  173.0 1.3 copy.10
